TPU v7x, 32 devices: a whole 2x2x4 slice. The times are simulated.
32 devices in a mesh: mesh: 8 (over z, core), band: 4 (over y, x).
Axes of the slice: x: 2, y: 2, z: 4, core: 2. Of those that a mesh axis runs over, the one named last changes fastest.
Arguments:
- filter_block: bfloat16 [512, 61440], P('band', 'mesh'), may hold values from -6 to 6
- local_pot: float32 [61440], P('mesh'), may hold values from 0.5 to 2
- cell_scale: float32 [1024], P('mesh'), may hold values from 0.5 to 2
- cell_kernel: bfloat16 [125, 125], replicated
- cell_map: int32 [125, 1024], P(None, 'mesh'), may hold values from 0 to 8191, as said below
- neighbour_ids: int32 [8, 6], P('mesh'), may hold values from 0 to 7, as said below
- send_nodes: int32 [8, 6, 64], P('mesh'), may hold values from 0 to 7679
- rotation_rows: bfloat16 [512, 512], P('band'), may hold values from -0.25 to 0.25
- panel_owner: int32 [2], replicated, may hold values from 0 to 3
Outputs:
- filtered: bfloat16 [512, 61440], P('band', 'mesh')
- rotated: bfloat16 [512, 61440], P(None, ('mesh', 'band'))
- state_energy: float32 [512], P('band')
Inputs may be any that keep to these rules, and one draw needn't show every extreme that they name: `neighbour_ids`: row p lists 6 distinct partitions other than p; q is listed in row p exactly when p is listed in row q. `cell_map`: in the columns of partition p's cells an entry below 7680 names an owned node of p, and an entry 7680 + q*64 + g names slot g of a partition q listed in row p of neighbour_ids.
All inputs are finite; a program needn't handle non-finite values.
Results may differ from a plain program's by a relative error of at most 0.0059.
Values may be sent and summed in bfloat16 or wider, within the bound.
A program may use at most 64 MiB of HBM per device.

v0:
```python
import jax
import jax.numpy as jnp
from jax import lax
from jax.sharding import PartitionSpec as P

center = 6.0
half_width = 4.0


def spread(value, axis, root):
    mine = lax.axis_index(axis) == root
    return lax.psum(jnp.where(mine, value, jnp.zeros_like(value)), axis)


def import_ghosts(state_field, neighbour_ids, send_nodes):
    count = state_field.shape[0]
    mesh_size = lax.axis_size("mesh")
    lists = send_nodes[0]
    packed = jnp.take(state_field, lists.reshape(-1), axis=1).reshape(
        count, lists.shape[0], lists.shape[1]
    )
    placement = (
        neighbour_ids[0][None, :] == jnp.arange(mesh_size, dtype=jnp.int32)[:, None]
    ).astype(jnp.bfloat16)
    outgoing = jnp.einsum("qr,srg->sqg", placement, packed, preferred_element_type=jnp.float32)
    outgoing = outgoing.astype(jnp.bfloat16).reshape(count, mesh_size * lists.shape[1])
    return lax.all_to_all(outgoing, "mesh", split_axis=1, concat_axis=1, tiled=True)


def apply_cells(state_field, ghosts, cell_map, cell_scale, cell_kernel, local_pot):
    count = state_field.shape[0]
    extended = jnp.concatenate([state_field, ghosts], axis=1)
    cells = cell_map.shape[1]
    width = 128

    def add_block(block_id, totals):
        gathered = jnp.take(extended, cell_map, axis=1)
        product = (
            jnp.einsum("ab,sbc->sac", cell_kernel, gathered, preferred_element_type=jnp.float32)
            * cell_scale
        )
        return totals.at[:, cell_map.reshape(-1)].add(product.reshape(count, -1))

    totals = lax.fori_loop(
        0, cells // width, add_block, jnp.zeros((count, extended.shape[1]), jnp.float32)
    )
    return totals[:, : state_field.shape[1]] + local_pot * state_field.astype(jnp.float32)


def per_device(
    filter_block,
    local_pot,
    cell_scale,
    cell_kernel,
    cell_map,
    neighbour_ids,
    send_nodes,
    rotation_rows,
    panel_owner,
):
    count = filter_block.shape[0]
    node_count = filter_block.shape[1]
    ghosts_zero = import_ghosts(filter_block, neighbour_ids, send_nodes)
    image_zero = apply_cells(
        filter_block, ghosts_zero, cell_map, cell_scale, cell_kernel, local_pot
    )
    start_field = filter_block.astype(jnp.float32)
    field_one = ((image_zero - center * start_field) / half_width).astype(jnp.bfloat16)
    ghosts_one = import_ghosts(field_one, neighbour_ids, send_nodes)
    image_one = apply_cells(field_one, ghosts_one, cell_map, cell_scale, cell_kernel, local_pot)
    one_float = field_one.astype(jnp.float32)
    energy_local = jnp.sum(one_float * image_one, axis=1)
    state_energy = lax.psum(energy_local, "mesh") / (node_count * lax.axis_size("mesh"))
    filtered = (2.0 * (image_one - center * one_float) / half_width - start_field).astype(
        jnp.bfloat16
    )
    band_index = lax.axis_index("band")
    totals = jnp.zeros((count, node_count), jnp.float32)
    for step_id in range(panel_owner.shape[0]):
        owner_id = panel_owner[step_id]
        panel_rows, coefficients = (
            spread(filtered, "band", owner_id),
            spread(rotation_rows, "band", owner_id),
        )
        my_coeff = lax.dynamic_slice_in_dim(coefficients, band_index * count, count, 1)
        totals = totals + lax.dot_general(
            my_coeff, panel_rows, (((0,), (0,)), ((), ())), preferred_element_type=jnp.float32
        )
    rotated = lax.all_to_all(
        totals.astype(jnp.bfloat16), "band", split_axis=1, concat_axis=0, tiled=True
    )
    return (filtered, rotated, state_energy)


def solution(mesh):
    placed = (
        P("band", "mesh"),
        P("mesh"),
        P("mesh"),
        P(),
        P(None, "mesh"),
        P("mesh", None),
        P("mesh", None, None),
        P("band", None),
        P(),
    )
    return jax.shard_map(
        per_device,
        mesh=mesh,
        in_specs=placed,
        out_specs=(P("band", "mesh"), P(None, ("mesh", "band")), P("band")),
        check_vma=False,
    )
```

profile of v0, /device:TPU:0, one launch (start us, length us, event | category | flops | bytes accessed | tf_op | source)
XLA Modules:
  0.0 498.6 jit_solution(12888701508582459800)
XLA Ops:
  7.2 0.0 copy-start
  7.2 0.0 copy-start.9
  7.2 0.0 copy-start.6
  7.2 0.0 copy-start.11
  7.2 0.7 reduce.1
  8.0 0.1 reshape_squeeze.4
  8.0 2.8 copy.43
  10.9 0.0 copy-start.3
  10.9 1.4 gather_fusion
  12.4 0.1 broadcast_select_fusion.5
  12.5 0.0 copy-done.9
  12.5 0.2 fusion.28
  12.7 0.7 copy.42
  13.4 6.3 %all-to-all-start = ((bf16[128,8,64]{0,2,1:T(8,128)(2,1)}), bf16[128,8,64]{0,2,1:T(8,128)(2,1)S(1)}, u32[]{:S(2)}, u32[]{:S(2)}) async-start(bf16[128,8,64]{0,2,1:T(8,128)(2,1)} %copy.42), calls=%async_computation | async-start | bytes 262144 | tf_op jit(solution)/shard_map/all_to_all | solution.py:27
  19.7 0.0 copy-done.6
  19.8 0.2 fusion.32
  20.0 0.0 copy-done.11
  20.0 0.6 fusion.49
  20.6 0.1 copy.38
  21.9 4.6 all-to-all-done
  26.5 0.0 copy-done.3
  26.5 1.7 pad_maximum_fusion
  28.2 33.0 %gather_fusion.1 = bf16[16000,128]{1,0:T(8,128)(2,1)} fusion(bf16[128,8192]{0,1:T(8,128)(2,1)S(1)} %pad_maximum_fusion, s32[16384]{0:T(1024)S(1)} %pad_clamp_fusion), kind=kCustom, calls=%fused_computation.1.clone | custom fusion | bytes 8256000 | tf_op jit(solution)/shard_map/while/body/eval_jaxpr/jit(_take)/gather | solution.py:37
  61.1 7.2 %copy.44 = bf16[125,128,128]{0,1,2:T(8,128)(2,1)} copy(bf16[125,128,128]{2,1,0:T(8,128)(2,1)} %bitcast.64) | data formatting | bytes 8192000 | tf_op jit(solution)/shard_map/while/body/eval_jaxpr/jit(_take)/gather | solution.py:37
  68.3 0.0 copy-done
  68.3 0.0 copy-done.10
  68.3 6.7 %multiply_bitcast_fusion.1 = f32[128,125,128]{1,2,0:T(8,128)} fusion(f32[128]{0:T(128)S(1)} %copy-done.10, bf16[125,128,128]{0,1,2:T(8,128)(2,1)} %copy.44, pred[125,128]{0,1:T(8,128)(4,1)S(1)} %copy.38, bf16[125,125]{1,0:T(8,128)(2,1)S(1)} %copy-done), kind=kOutput, calls=%fused_computation.9 | convolution fusion | flops 516096000 | bytes 12335762 | tf_op jit(solution)/shard_map/while/body/eval_jaxpr/ab,sbc->sac/dot_general | solution.py:39
  75.0 9.5 %copy.45 = f32[128,125,128]{0,2,1:T(8,128)} copy(f32[128,125,128]{1,2,0:T(8,128)} %multiply_bitcast_fusion.1) | data formatting | bytes 16384000 | tf_op jit(solution)/shard_map/while/body/eval_jaxpr/mul | solution.py:39
  84.5 90.1 %scatter_custom_fusion = f32[128,8192]{0,1:T(8,128)} fusion(s32[16000]{0:T(1024)S(1)} %fusion.32, f32[16000,128]{1,0:T(8,128)} %bitcast.66, f32[]{:T(128)} %constant.27.clone.1), kind=kCustom, calls=%fused_computation.39 | custom fusion | flops 2048000 | bytes 4194816 | tf_op jit(solution)/shard_map/while/body/eval_jaxpr/scatter-add | solution.py:42
  174.6 0.0 copy-done.7
  174.6 5.1 %fusion.12 = bf16[128,7680]{0,1:T(8,128)(2,1)S(1)} fusion(bf16[128,7680]{0,1:T(8,128)(2,1)} %copy-done.3, f32[128,8192]{0,1:T(8,128)} %scatter_custom_fusion, f32[7680]{0:T(1024)S(1)} %copy-done.7), kind=kLoop, calls=%fused_computation.27 | loop fusion | flops 6881280 | bytes 7895040 | tf_op jit(solution)/shard_map/convert_element_type | solution.py:68
  179.7 0.0 copy-start.1
  179.7 1.4 gather_fusion.2
  181.2 0.1 broadcast_select_fusion.4
  181.3 0.2 fusion.29
  181.5 0.7 copy.48
  182.1 3.4 all-to-all-start.1
  185.5 0.2 all-reduce.3.cloned.1.call-start
  185.7 0.0 copy-done.8
  185.7 0.7 broadcast_select_fusion.2
  186.5 5.7 %all-to-all-done.1 = bf16[128,8,64]{0,2,1:T(8,128)(2,1)S(1)} async-done(((bf16[128,8,64]{0,2,1:T(8,128)(2,1)}), bf16[128,8,64]{0,2,1:T(8,128)(2,1)S(1)}, u32[]{:S(2)}, u32[]{:S(2)}) %all-to-all-start.1) | async-done | bytes 131104 | tf_op jit(solution)/shard_map/all_to_all | solution.py:27
  192.2 0.0 copy-done.1
  192.2 1.7 pad_maximum_fusion.1
  193.9 33.0 %gather_fusion.3 = bf16[16000,128]{1,0:T(8,128)(2,1)} fusion(bf16[128,8192]{0,1:T(8,128)(2,1)S(1)} %pad_maximum_fusion.1, s32[16384]{0:T(1024)S(1)} %pad_clamp_fusion), kind=kCustom, calls=%fused_computation.3.clone | custom fusion | bytes 8256000 | tf_op jit(solution)/shard_map/while/body/eval_jaxpr/jit(_take)/gather | solution.py:37
  226.9 7.2 %copy.49 = bf16[125,128,128]{0,1,2:T(8,128)(2,1)} copy(bf16[125,128,128]{2,1,0:T(8,128)(2,1)} %bitcast.63) | data formatting | bytes 8192000 | tf_op jit(solution)/shard_map/while/body/eval_jaxpr/jit(_take)/gather | solution.py:37
  234.0 6.7 %multiply_bitcast_fusion = f32[128,125,128]{1,2,0:T(8,128)} fusion(f32[128]{0:T(128)S(1)} %copy-done.10, bf16[125,128,128]{0,1,2:T(8,128)(2,1)} %copy.49, pred[125,128]{0,1:T(8,128)(4,1)S(1)} %copy.38, bf16[125,125]{1,0:T(8,128)(2,1)S(1)} %copy-done), kind=kOutput, calls=%fused_computation.8 | convolution fusion | flops 516096000 | bytes 12335762 | tf_op jit(solution)/shard_map/while/body/eval_jaxpr/ab,sbc->sac/dot_general | solution.py:39
  240.7 9.5 %copy.50 = f32[128,125,128]{0,2,1:T(8,128)} copy(f32[128,125,128]{1,2,0:T(8,128)} %multiply_bitcast_fusion) | data formatting | bytes 16384000 | tf_op jit(solution)/shard_map/while/body/eval_jaxpr/mul | solution.py:39
  250.2 90.2 %scatter_custom_fusion.1 = f32[128,8192]{0,1:T(8,128)} fusion(s32[16000]{0:T(1024)S(1)} %fusion.32, f32[16000,128]{1,0:T(8,128)} %bitcast.65, f32[]{:T(128)} %constant.27.clone.1), kind=kCustom, calls=%fused_computation.37 | custom fusion | flops 2048000 | bytes 4194816 | tf_op jit(solution)/shard_map/while/body/eval_jaxpr/scatter-add | solution.py:42
  340.4 6.3 %broadcast_select_fusion = (bf16[128,7680]{0,1:T(8,128)(2,1)}, bf16[128,7680]{0,1:T(8,128)(2,1)S(1)}) fusion(pred[]{:T(512)S(6)} %eq.17, bf16[128,7680]{0,1:T(8,128)(2,1)} %copy-done.3, bf16[128,7680]{0,1:T(8,128)(2,1)S(1)} %copy-done.2, f32[7680]{0:T(1024)S(1)} %copy-done.7, f32[128,8192]{0,1:T(8,128)} %scatter_custom_fusion.1), kind=kLoop, calls=%fused_computation.42 | loop fusion | flops 9830400 | bytes 11827201 | tf_op jit(solution)/shard_map/jit(_where)/select_n | solution.py:12
  346.7 1.3 copy-done.4
  348.0 1.4 broadcast_select_fusion.1
  349.4 0.0 all-reduce.3.cloned.1.call-update
  349.4 104.1 %all-reduce.3.cloned.1.call-done = (bf16[128,7680]{0,1:T(8,128)(2,1)}, bf16[128,512]{1,0:T(8,128)(2,1)}, bf16[128,7680]{0,1:T(8,128)(2,1)}, bf16[128,512]{1,0:T(8,128)(2,1)}) async-done(((bf16[128,7680]{0,1:T(8,128)(2,1)}, bf16[128,512]{1,0:T(8,128)(2,1)}, bf16[128,7680]{0,1:T(8,128)(2,1)}, bf16[128,512]{1,0:T(8,128)(2,1)}), (bf16[128,7680]{0,1:T(8,128)(2,1)}, bf16[128,512]{1,0:T(8,128)(2,1)}, ...) | async-done | bytes 4194320 | tf_op jit(solution)/shard_map/psum | solution.py:12
  453.5 2.4 fusion.37
  455.9 0.0 copy-done.5
  455.9 1.5 fusion
  457.4 1.4 copy.61
  458.8 4.4 all-to-all-start.2
  463.2 4.0 copy.52
  467.2 4.7 fusion.17
  471.9 16.4 %psum.39 = f32[128]{0:T(128)S(1)} all-reduce(f32[128]{0:T(128)S(1)} %fusion.17), channel_id=1, replica_groups=mesh['mesh'=8,'band'=4] {'mesh'}, use_global_device_ids=true, to_apply=%region_7.10 | all-reduce | flops 128 | bytes 1024 | tf_op jit(solution)/shard_map/psum | solution.py:73
  488.3 0.5 broadcast_multiply_fusion
  488.8 0.0 all-to-all-done.2
  488.8 3.0 copy.67
  (13 shorter events, 0.1 us)
Async XLA Ops:
  7.2 61.1 %copy-start = (bf16[125,125]{1,0:T(8,128)(2,1)S(1)}, bf16[125,125]{1,0:T(8,128)(2,1)}, u32[]{:S(2)}) copy-start(bf16[125,125]{1,0:T(8,128)(2,1)} %param.16) | copy-start | bytes 93754
  7.2 5.3 %copy-start.9 = (s32[1,6]{1,0:T(1,128)S(1)}, s32[1,6]{1,0:T(1,128)}, u32[]{:S(2)}) copy-start(s32[1,6]{1,0:T(1,128)} %param.18) | copy-start | bytes 76
  7.2 12.5 %copy-start.6 = (s32[125,128]{1,0:T(8,128)S(1)}, s32[125,128]{1,0:T(8,128)}, u32[]{:S(2)}) copy-start(s32[125,128]{1,0:T(8,128)} %param.17) | copy-start | bytes 192004
  7.2 12.8 %copy-start.11 = (s32[2]{0:T(128)S(1)}, s32[2]{0:T(128)}, u32[]{:S(2)}) copy-start(s32[2]{0:T(128)} %param.21) | copy-start | bytes 28
  10.9 15.6 %copy-start.3 = (bf16[128,7680]{0,1:T(8,128)(2,1)}, bf16[128,7680]{0,1:T(8,128)(2,1)S(1)}, u32[]{:S(2)}) copy-start(bf16[128,7680]{0,1:T(8,128)(2,1)S(1)} %copy.43) | copy-start | bytes 5898244
  13.4 13.1 %all-to-all-start = ((bf16[128,8,64]{0,2,1:T(8,128)(2,1)}), bf16[128,8,64]{0,2,1:T(8,128)(2,1)S(1)}, u32[]{:S(2)}, u32[]{:S(2)}) async-start(bf16[128,8,64]{0,2,1:T(8,128)(2,1)} %copy.42), calls=%async_computation | async-start | bytes 262144 | tf_op jit(solution)/shard_map/all_to_all | solution.py:27
  61.1 7.2 %copy-start.10 = (f32[128]{0:T(128)S(1)}, f32[128]{0:T(128)}, u32[]{:S(2)}) copy-start(f32[128]{0:T(128)} %param.15) | copy-start | bytes 1540
  84.5 90.1 %copy-start.7 = (f32[7680]{0:T(1024)S(1)}, f32[7680]{0:T(1024)}, u32[]{:S(2)}) copy-start(f32[7680]{0:T(1024)} %param.14) | copy-start | bytes 92164
  174.6 11.2 %copy-start.8 = (bf16[128,512]{1,0:T(8,128)(2,1)S(1)}, bf16[128,512]{1,0:T(8,128)(2,1)}, u32[]{:S(2)}) copy-start(bf16[128,512]{1,0:T(8,128)(2,1)} %param.20) | copy-start | bytes 393220
  179.7 12.5 %copy-start.1 = (bf16[128,7680]{0,1:T(8,128)(2,1)}, bf16[128,7680]{0,1:T(8,128)(2,1)S(1)}, u32[]{:S(2)}) copy-start(bf16[128,7680]{0,1:T(8,128)(2,1)S(1)} %fusion.12) | copy-start | bytes 5898244
  182.1 10.1 %all-to-all-start.1 = ((bf16[128,8,64]{0,2,1:T(8,128)(2,1)}), bf16[128,8,64]{0,2,1:T(8,128)(2,1)S(1)}, u32[]{:S(2)}, u32[]{:S(2)}) async-start(bf16[128,8,64]{0,2,1:T(8,128)(2,1)} %copy.48), calls=%async_computation.1 | async-start | bytes 262144 | tf_op jit(solution)/shard_map/all_to_all | solution.py:27
  185.5 268.0 %all-reduce.3.cloned.1.call-start = ((), (), s32[]{:S(2)}) async-start(), calls=%async_computation.3 | async-start | bytes 8388608 | tf_op jit(solution)/shard_map/psum | solution.py:12
  250.2 90.2 %copy-start.2 = (bf16[128,7680]{0,1:T(8,128)(2,1)S(1)}, bf16[128,7680]{0,1:T(8,128)(2,1)}, u32[]{:S(2)}) copy-start(bf16[128,7680]{0,1:T(8,128)(2,1)} %copy-done.1) | copy-start | bytes 5898244
  346.7 1.3 copy-start.4
  453.5 2.4 copy-start.5
  458.8 30.0 %all-to-all-start.2 = ((bf16[128,4,1920]{2,0,1:T(8,128)(2,1)}), bf16[128,4,1920]{2,0,1:T(8,128)(2,1)}, u32[]{:S(2)}, u32[]{:S(2)}) async-start(bf16[128,4,1920]{2,0,1:T(8,128)(2,1)} %bitcast.67), calls=%async_computation.2 | async-start | bytes 3932160 | tf_op jit(solution)/shard_map/all_to_all | solution.py:89
Sparse Core Ops, SparseCore 0:
  349.5 103.8 all-reduce.2
where the time goes:
time: 500 us; the launch traced here: 499 us
  other arithmetic  204 us (41%)
  local copies, waits for them, and re-layouts  117 us (23%)
  waiting for transfers between devices  114 us (23%)
  matrix products  17.6 us (4%)
  blocking collectives  16.4 us (3%)
  between operations  15.5 us (3%)
  starting transfers between devices  14.3 us (3%)
    scatter-add x2, other arithmetic, add_block(): return totals.at[:, cell_map.reshape(-1)].add(product.reshape(count, -1))  180 us
    psum x1, waiting for transfers between devices, spread(): return lax.psum(jnp.where(mine, value, jnp.zeros_like(value)), axis)  104 us
    gather x4, local copies, waits for them, and re-layouts, add_block(): gathered = jnp.take(extended, cell_map, axis=1)  80.3 us
    mul x2, local copies, waits for them, and re-layouts, add_block(): jnp.einsum('ab,sbc->sac', cell_kernel, gathered, preferred_element_type=j...  19 us
    psum x1, blocking collectives, per_device(): lax.psum(energy_local, 'mesh') / (node_count * lax.axis_size('mesh'))  16.4 us
    dot_general x2, matrix products, add_block(): jnp.einsum('ab,sbc->sac', cell_kernel, gathered, preferred_element_type=j...  13.3 us
    unnamed x27, local copies, waits for them, and re-layouts  11.1 us
    all_to_all x2, waiting for transfers between devices, import_ghosts(): lax.all_to_all(outgoing, 'mesh', split_axis=1, concat_axis=1, tiled=True)  10.3 us
  transfers between devices with their start and end apart: 4, of which 3 were waited for; matrix products, arithmetic and copies ran while one was open for 2% of the time, Pallas kernels for 0%

commit v1 on v0

v1 whole, which is shorter than its diff:
```python
import functools

import jax
import jax.numpy as jnp
from jax import lax
from jax.experimental import pallas as pl
from jax.experimental.pallas import tpu as pltpu
from jax.sharding import PartitionSpec as P

center = 6.0
half_width = 4.0
LANES = 128
TABLES = 8
VMEM_BYTES = 56 * 1024 * 1024


def flat(ref):
    return ref.reshape(ref.shape[0], ref.shape[2])


def pack_rows(rows_ref, ids_ref, send_ref, packed_ref, out_ref):
    out_ref[...] = jnp.zeros_like(out_ref)
    slots = out_ref.shape[1]

    @pl.loop(0, ids_ref.shape[1])
    def _(r):
        for g in range(slots):
            packed_ref[g] = rows_ref[send_ref[r, g]]
        out_ref[ids_ref[0, r]] = flat(packed_ref)[...].astype(out_ref.dtype)


def apply_cells(map_ref, scale_ref, kernel_ref, pot_ref, own_ref, ghost_ref, ext, tables, gathers, products):
    nodes = own_ref.shape[0]
    npe, cells = map_ref.shape
    parts, slots, _ = ghost_ref.shape

    @pl.loop(0, nodes // LANES)
    def _(i):
        at = pl.ds(pl.multiple_of(i * LANES, LANES), LANES)
        block = own_ref[at, :]
        flat(ext)[at, :] = block.astype(jnp.float32)
        row = lax.broadcasted_iota(jnp.int32, (LANES, LANES), 0)
        column = lax.broadcasted_iota(jnp.int32, (LANES, LANES), 1)
        shifted = pot_ref[pl.ds(i, 1), :] - center
        diagonal = jnp.where(row == column, shifted, 0.0)
        high = diagonal.astype(jnp.bfloat16)
        low = (diagonal - high.astype(jnp.float32)).astype(jnp.bfloat16)
        flat(tables[0])[at, :] = jnp.dot(high, block, preferred_element_type=jnp.float32) + jnp.dot(
            low, block, preferred_element_type=jnp.float32
        )
        for table in tables[1:]:
            flat(table)[at, :] = jnp.zeros((LANES, table.shape[2]), jnp.float32)

    @pl.loop(0, parts)
    def _(q):
        start = pl.multiple_of(nodes + q * slots, slots)
        flat(ext)[pl.ds(start, slots), :] = ghost_ref[q].astype(jnp.float32)
        for table in tables:
            flat(table)[pl.ds(start, slots), :] = jnp.zeros((slots, table.shape[2]), jnp.float32)

    for ref in (*gathers, *products):
        ref[...] = jnp.zeros_like(ref)

    def stage(step, gather_out, gather_in, product_out, product_in):
        last = cells - 1
        take = jnp.minimum(step, last)
        middle = jnp.clip(step - 1, 0, last)
        put = jnp.clip(step - 2, 0, last)
        flat(product_out)[...] = (
            jnp.dot(kernel_ref[...], flat(gather_in)[...].astype(jnp.bfloat16), preferred_element_type=jnp.float32)
            * scale_ref[middle]
        )
        for first in range(0, npe, TABLES):
            group = range(first, min(first + TABLES, npe))
            rows = [ext[map_ref[b, take]] for b in group]
            where_to = [map_ref[a, put] for a in group]
            sums = [tables[a - first][at] + product_in[a] for a, at in zip(group, where_to)]
            for a, at, value in zip(group, where_to, sums):
                tables[a - first][at] = value
            for b, row in zip(group, rows):
                gather_out[b] = row

    @pl.loop(0, (cells + 3) // 2)
    def _(pair):
        stage(2 * pair, gathers[0], gathers[1], products[1], products[0])
        stage(2 * pair + 1, gathers[1], gathers[0], products[0], products[1])


def table_sum(tables, at):
    values = [flat(table)[at, :] for table in tables]
    while len(values) > 1:
        values = [a + b for a, b in zip(values[::2], values[1::2])]
    return values[0]


def first_kernel(
    map_ref, scale_ref, ids_ref, send_ref, kernel_ref, pot_ref, own_ref, ghost_ref,
    one_out, packed_out, ext, packed, *scratch,
):
    tables, gathers, products = scratch[:TABLES], scratch[TABLES : TABLES + 2], scratch[TABLES + 2 :]
    apply_cells(map_ref, scale_ref, kernel_ref, pot_ref, own_ref, ghost_ref, ext, tables, gathers, products)

    @pl.loop(0, own_ref.shape[0] // LANES)
    def _(i):
        at = pl.ds(pl.multiple_of(i * LANES, LANES), LANES)
        one = (table_sum(tables, at) * (1.0 / half_width)).astype(jnp.bfloat16)
        one_out[at, :] = one
        flat(ext)[at, :] = one.astype(jnp.float32)

    pack_rows(ext, ids_ref, send_ref, packed, packed_out)


def second_kernel(
    map_ref, scale_ref, kernel_ref, pot_ref, own_ref, ghost_ref, field_ref,
    filtered_out, pieces_out, energy_out, ext, *scratch,
):
    tables, gathers, products = scratch[:TABLES], scratch[TABLES : TABLES + 2], scratch[TABLES + 2 :]
    apply_cells(map_ref, scale_ref, kernel_ref, pot_ref, own_ref, ghost_ref, ext, tables, gathers, products)
    count = own_ref.shape[1]
    piece = pieces_out.shape[2] // LANES
    energy_out[...] = jnp.zeros_like(energy_out)

    @pl.loop(0, pieces_out.shape[0])
    def _(band):
        @pl.loop(0, piece)
        def _(j):
            here = pl.ds(pl.multiple_of(j * LANES, LANES), LANES)
            at = pl.ds(pl.multiple_of((band * piece + j) * LANES, LANES), LANES)
            total = table_sum(tables, at)
            one = flat(ext)[at, :]
            terms = one * (total + center * one)
            energy_out[...] += jnp.sum(terms.reshape(LANES // 8, 8, count), axis=0)
            turned = (total * (2.0 / half_width)).T
            value = (turned - field_ref[:, at].astype(jnp.float32)).astype(jnp.bfloat16)
            filtered_out[:, at] = value
            pieces_out[band, :, here] = value


def peer_at(axis, step):
    return lax.rem(lax.axis_index(axis) + step, lax.axis_size(axis))


def greet(axes):
    barrier = pltpu.get_barrier_semaphore()
    peers = 0
    for axis in axes:
        for step in range(1, lax.axis_size(axis)):
            pl.semaphore_signal(
                barrier, inc=1, device_id={axis: peer_at(axis, step)}, device_id_type=pl.DeviceIdType.MESH
            )
            peers += 1
    pl.semaphore_wait(barrier, peers)


def send(source, target, axis, step, send_sem, recv_sem):
    copy = pltpu.make_async_remote_copy(
        src_ref=source,
        dst_ref=target,
        send_sem=send_sem.at[step - 1],
        recv_sem=recv_sem.at[step - 1],
        device_id={axis: peer_at(axis, step)},
        device_id_type=pl.DeviceIdType.MESH,
    )
    copy.start()
    return copy


def turn_kernel(
    ids_ref, send_ref, field_ref, rotation_ref, rows_out, ghost_out, rotation_out,
    rows, packed, outgoing, send_sem, recv_sem, send_more, recv_more,
):
    nodes = field_ref.shape[1]
    parts, slots, _ = outgoing.shape
    band, me = lax.axis_index("band"), lax.axis_index("mesh")
    greet(("band", "mesh"))
    copies = [
        send(rotation_ref, rotation_out.at[band], "band", step, send_more, recv_more)
        for step in range(1, lax.axis_size("band"))
    ]
    rotation_out[band] = rotation_ref[...]

    @pl.loop(0, nodes // LANES)
    def _(i):
        at = pl.ds(pl.multiple_of(i * LANES, LANES), LANES)
        block = field_ref[:, at].astype(jnp.float32).T
        rows[at, :] = block
        rows_out[at, :] = block.astype(jnp.bfloat16)

    @pl.loop(0, parts)
    def _(q):
        place = jnp.int32(0)
        listed = jnp.int32(0)
        for r in range(ids_ref.shape[1]):
            same = ids_ref[0, r] == q
            place = jnp.where(same, r, place)
            listed = jnp.where(same, 1, listed)
        for g in range(slots):
            packed[g : g + 1, :] = rows[pl.ds(send_ref[place, g], 1), :]
        outgoing[q] = (packed[...] * listed.astype(jnp.float32)).astype(outgoing.dtype)

    copies += [
        send(outgoing.at[peer_at("mesh", step)], ghost_out.at[me], "mesh", step, send_sem, recv_sem)
        for step in range(1, lax.axis_size("mesh"))
    ]
    ghost_out[me] = jnp.zeros(ghost_out.shape[1:], ghost_out.dtype)
    for copy in copies:
        copy.wait()


def exchange_kernel(packed_ref, ghost_out, send_sem, recv_sem):
    me = lax.axis_index("mesh")
    greet(("mesh",))
    copies = [
        send(packed_ref.at[peer_at("mesh", step)], ghost_out.at[me], "mesh", step, send_sem, recv_sem)
        for step in range(1, lax.axis_size("mesh"))
    ]
    ghost_out[me] = jnp.zeros(ghost_out.shape[1:], ghost_out.dtype)
    for copy in copies:
        copy.wait()


def swap_kernel(pieces_ref, energy_ref, pieces_out, energy_out, keep_sem, send_sem, recv_sem, send_small, recv_small):
    band, me = lax.axis_index("band"), lax.axis_index("mesh")
    greet(("band", "mesh"))
    copies = [
        send(pieces_ref.at[peer_at("band", step)], pieces_out.at[band], "band", step, send_sem, recv_sem)
        for step in range(1, lax.axis_size("band"))
    ]
    copies += [
        send(energy_ref, energy_out.at[me], "mesh", step, send_small, recv_small)
        for step in range(1, lax.axis_size("mesh"))
    ]
    keep = pltpu.make_async_copy(pieces_ref.at[band], pieces_out.at[band], keep_sem)
    keep.start()
    energy_out[me] = energy_ref[...]
    for copy in copies:
        copy.wait()
    keep.wait()


def rotate_kernel(nodes_all, block, owner_ref, rotations, pieces_ref, energy_ref, out_ref, energy_out):
    steps = owner_ref.shape[0]
    rotation = jnp.concatenate([rotations[owner_ref[k]] for k in range(steps)], axis=0)
    turned = rotation.astype(jnp.float32).T.astype(jnp.bfloat16)
    parts = jnp.sum(energy_ref[...], axis=0)
    energy_out[...] = jnp.sum(parts, axis=0, keepdims=True) / nodes_all

    @pl.loop(0, pieces_ref.shape[2] // block)
    def _(j):
        at = pl.ds(pl.multiple_of(j * block, block), block)
        panel = jnp.concatenate([pieces_ref[owner_ref[k], :, at] for k in range(steps)], axis=0)
        out_ref[:, at] = jnp.dot(turned, panel, preferred_element_type=jnp.float32).astype(out_ref.dtype)


vmem = pl.BlockSpec(memory_space=pltpu.VMEM)
smem = pl.BlockSpec(memory_space=pltpu.SMEM)


anywhere = pl.BlockSpec(memory_space=pl.ANY)


def call(body, name, outs, in_specs, out_specs=None, scratch=(), traffic=None, collective=None):
    return pl.pallas_call(
        body,
        name=name,
        out_shape=outs,
        in_specs=in_specs,
        out_specs=out_specs or tuple(vmem for _ in outs),
        scratch_shapes=list(scratch),
        cost_estimate=traffic and pl.CostEstimate(flops=traffic, bytes_accessed=traffic, transcendentals=0),
        compiler_params=pltpu.CompilerParams(
            vmem_limit_bytes=VMEM_BYTES,
            collective_id=collective,
            has_side_effects=collective is not None,
        ),
    )


def per_device(
    filter_block, local_pot, cell_scale, cell_kernel, cell_map, neighbour_ids, send_nodes, rotation_rows, panel_owner
):
    count, nodes = filter_block.shape
    mesh_size, band_size = lax.axis_size("mesh"), lax.axis_size("band")
    slots = send_nodes.shape[2]
    extent = nodes + mesh_size * slots
    npe, cells = cell_map.shape
    side = -(-npe // LANES) * LANES
    lists = send_nodes[0]
    kernel = jnp.pad(cell_kernel, ((0, side - npe), (0, side - npe)))
    pot = local_pot.reshape(nodes // LANES, LANES)
    shape = jax.ShapeDtypeStruct
    f32, bf16 = jnp.float32, jnp.bfloat16
    width = nodes // band_size
    block = 3 * LANES if width % (3 * LANES) == 0 else LANES
    traffic = 5 * 4 * npe * cells * count

    def table(rows):
        return pltpu.VMEM((rows, 1, count), f32)

    rows = shape((nodes, count), bf16)
    packed = shape((mesh_size, slots, count), bf16)
    working = [table(extent) for _ in range(TABLES)] + [table(side) for _ in range(4)]
    dma = pltpu.SemaphoreType.DMA

    def exchange(outgoing, collective):
        sems = dma((mesh_size - 1,))
        return call(exchange_kernel, "exchange", (packed,), [vmem], scratch=[sems, sems], collective=collective)(
            outgoing
        )[0]

    all_rotations = shape((band_size, *rotation_rows.shape), bf16)
    zero, ghosts, rotations = call(
        turn_kernel,
        "turn",
        (rows, packed, all_rotations),
        [smem, smem, vmem, vmem],
        scratch=[
            pltpu.VMEM((nodes, count), f32),
            pltpu.VMEM((slots, count), f32),
            pltpu.VMEM((mesh_size, slots, count), bf16),
            *[dma((mesh_size - 1,))] * 2,
            *[dma((band_size - 1,))] * 2,
        ],
        collective=0,
    )(neighbour_ids, lists, filter_block, rotation_rows)
    one, outgoing = call(
        first_kernel,
        "first",
        (rows, packed),
        [smem] * 4 + [vmem] * 4,
        scratch=[table(extent), table(slots), *working],
        traffic=traffic,
    )(cell_map, cell_scale, neighbour_ids, lists, kernel, pot, zero, ghosts)
    all_pieces = shape((band_size, count, width), bf16)
    filtered, pieces, energy = call(
        second_kernel,
        "second",
        (shape((count, nodes), bf16), all_pieces, shape((8, count), f32)),
        [smem] * 2 + [vmem] * 5,
        scratch=[table(extent), *working],
        traffic=traffic,
    )(cell_map, cell_scale, kernel, pot, one, exchange(outgoing, 1), filter_block)
    pieces, energy = call(
        swap_kernel,
        "swap",
        (all_pieces, shape((mesh_size, 8, count), f32)),
        [anywhere, vmem],
        out_specs=(anywhere, vmem),
        scratch=[dma(()), *[dma((band_size - 1,))] * 2, *[dma((mesh_size - 1,))] * 2],
        collective=2,
    )(pieces, energy)
    rotated, energy = call(
        functools.partial(rotate_kernel, nodes * mesh_size, block),
        "rotate",
        (shape((rotation_rows.shape[1], width), bf16), shape((1, count), f32)),
        [smem, vmem, vmem, vmem],
    )(panel_owner, rotations, pieces, energy)
    return (filtered, rotated, energy[0])


def solution(mesh):
    placed = (
        P("band", "mesh"),
        P("mesh"),
        P("mesh"),
        P(),
        P(None, "mesh"),
        P("mesh", None),
        P("mesh", None, None),
        P("band", None),
        P(),
    )
    return jax.shard_map(
        per_device,
        mesh=mesh,
        in_specs=placed,
        out_specs=(P("band", "mesh"), P(None, ("mesh", "band")), P("band")),
        check_vma=False,
    )
```

time: 500 us -> 177 us (0.35)
  other arithmetic: 204 us -> 0 us
  Pallas kernels: 0 us -> 173 us
  local copies, waits for them, and re-layouts: 117 us -> 2.64 us
  waiting for transfers between devices: 114 us -> 0 us
  matrix products: 17.6 us -> 0 us
  blocking collectives: 16.4 us -> 0 us
  between operations: 15.5 us -> 0.66 us
  starting transfers between devices: 14.3 us -> 0 us
    scatter-add x2 -> x0, other arithmetic: 180 us -> none  [add_block(): return totals.at[:, cell_map.reshape(-1)].add(product.reshape(count, -1))]
    pallas_call x0 -> x6, Pallas kernels: none -> 173 us  [the longest x1 59.3 us: per_device(): call(second_kernel, 'second', (shape((count, nodes), bf16), all_pieces, s...]
    psum x1 -> x0, waiting for transfers between devices: 104 us -> none  [spread(): return lax.psum(jnp.where(mine, value, jnp.zeros_like(value)), axis)]
    gather x6 -> x0, local copies, waits for them, and re-layouts: 83.2 us -> none  [the longest x4 80.3 us: add_block(): gathered = jnp.take(extended, cell_map, axis=1)]
    mul x2 -> x0, local copies, waits for them, and re-layouts: 19 us -> none  [add_block(): jnp.einsum('ab,sbc->sac', cell_kernel, gathered, preferred_element_type=j...]
    dot_general x6 -> x0, matrix products: 17.6 us -> none  [the longest x2 13.3 us: add_block(): jnp.einsum('ab,sbc->sac', cell_kernel, gathered, preferred_element_type=j...]
    psum x1 -> x0, blocking collectives: 16.4 us -> none  [per_device(): lax.psum(energy_local, 'mesh') / (node_count * lax.axis_size('mesh'))]
    all_to_all x3 -> x0, starting transfers between devices: 14.1 us -> none  [the longest x2 9.69 us: import_ghosts(): lax.all_to_all(outgoing, 'mesh', split_axis=1, concat_axis=1, tiled=True)]
  transfers between devices with their start and end apart: 4 -> 0, of which waited for: 3 -> 0; matrix products, arithmetic and copies ran while one was open for 2% -> 0% of each run, Pallas kernels for 0% -> 0%
where the time goes in v1:
time: 177 us
  Pallas kernels  173 us (98%)
  local copies, waits for them, and re-layouts  2.64 us (1%)
    pallas_call x1, Pallas kernels, per_device(): call(second_kernel, 'second', (shape((count, nodes), bf16), all_pieces, s...  59.3 us
    pallas_call x1, Pallas kernels, per_device(): call(first_kernel, 'first', (rows, packed), [smem] * 4 + [vmem] * 4, scra...  54 us
    pallas_call x1, Pallas kernels, per_device(): call(swap_kernel, 'swap', (all_pieces, shape((mesh_size, 8, count), f32))...  28.7 us
    pallas_call x1, Pallas kernels, per_device(): call(turn_kernel, 'turn', (rows, packed, all_rotations), [smem, smem, vme...  19.2 us
    pallas_call x1, Pallas kernels, exchange(): call(exchange_kernel, 'exchange', (packed,), [vmem], scratch=[sems, sems]...  7.76 us
    pallas_call x1, Pallas kernels, per_device(): call(functools.partial(rotate_kernel, nodes * mesh_size, block), 'rotate'...  4.55 us

profile of v1, /device:TPU:0, one launch (start us, length us, event | category | flops | bytes accessed | tf_op | source)
XLA Modules:
  0.0 176.8 jit_solution(12827153195531551483)
XLA Ops:
  0.6 1.3 copy.14
  1.9 1.4 pad.4.kernel_ref
  3.3 19.2 %turn.1 = (bf16[7680,128]{1,0:T(8,128)(2,1)}, bf16[8,64,128]{2,1,0:T(8,128)(2,1)}, bf16[4,128,512]{2,1,0:T(8,128)(2,1)}) custom-call(s32[1,6]{1,0:T(1,128)} %ids_ref.3, s32[6,64]{1,0:T(8,128)} %bitcast.7, bf16[128,7680]{1,0:T(8,128)(2,1)} %field_ref.3, bf16[128,512]{1,0:T(8,128)(2,1)} %rotation_ref.1), custom_call_target="tpu_custom_call" | custom-call | tf_op jit(solution)/shard_map/turn/pallas_call | solution.py:312
  22.5 54.0 %first.1 = (bf16[7680,128]{1,0:T(8,128)(2,1)}, bf16[8,64,128]{2,1,0:T(8,128)(2,1)}) custom-call(s32[125,128]{1,0:T(8,128)} %map_ref.3, f32[128]{0:T(128)} %scale_ref.3, s32[1,6]{1,0:T(1,128)} %ids_ref.3, s32[6,64]{1,0:T(8,128)} %bitcast.8, bf16[128,128]{1,0:T(8,128)(2,1)} %pad.4.kernel_ref, f32[60,128]{1,0:T(8,128)} %bitcast.5, ...), custom_call_target="tpu_custom_call" | custom-call | flops 40960000 | bytes 40960000 | tf_op jit(solution)/shard_map/first/pallas_call | solution.py:326
  76.5 7.8 %exchange.1.ghost_ref = bf16[8,64,128]{2,1,0:T(8,128)(2,1)} custom-call(bf16[8,64,128]{2,1,0:T(8,128)(2,1)} %get-tuple-element.18.packed_ref), custom_call_target="tpu_custom_call" | custom-call | tf_op jit(solution)/shard_map/exchange/pallas_call | solution.py:307
  84.2 59.3 %second.1 = (bf16[128,7680]{1,0:T(8,128)(2,1)}, bf16[4,128,1920]{2,1,0:T(8,128)(2,1)}, f32[8,128]{1,0:T(8,128)}) custom-call(s32[125,128]{1,0:T(8,128)} %map_ref.3, f32[128]{0:T(128)} %scale_ref.3, bf16[128,128]{1,0:T(8,128)(2,1)} %pad.4.kernel_ref, f32[60,128]{1,0:T(8,128)} %bitcast.6, bf16[7680,128]{1,0:T(8,128)(2,1)} %get-tuple-element.17.own_ref, ...), custom_call_target="tpu_custom_call" | custom-call | flops 40960000 | bytes 40960000 | tf_op jit(solution)/shard_map/second/pallas_call | solution.py:335
  143.5 28.7 %swap.1 = (bf16[4,128,1920]{2,1,0:T(8,128)(2,1)}, f32[8,8,128]{2,1,0:T(8,128)}) custom-call(bf16[4,128,1920]{2,1,0:T(8,128)(2,1)} %get-tuple-element.21.pieces_ref, f32[8,128]{1,0:T(8,128)} %get-tuple-element.22.energy_ref), custom_call_target="tpu_custom_call" | custom-call | tf_op jit(solution)/shard_map/swap/pallas_call | solution.py:343
  172.2 4.6 %rotate.1 = (bf16[512,1920]{1,0:T(8,128)(2,1)}, f32[1,128]{1,0:T(1,128)}) custom-call(s32[2]{0:T(128)} %owner_ref.1, bf16[4,128,512]{2,1,0:T(8,128)(2,1)} %get-tuple-element.20.rotations, bf16[4,128,1920]{2,1,0:T(8,128)(2,1)} %get-tuple-element.23.pieces_ref, f32[8,8,128]{2,1,0:T(8,128)} %get-tuple-element.24.energy_ref), custom_call_target="tpu_custom_call" | custom-call | tf_op jit(solution)/shard_map/rotate/pallas_call | solution.py:352
